TPU v7x, 128 devices: a whole 4x4x4 slice. The times are simulated.
128 devices in a mesh: slab: 32 (over x, y, core), lane: 4 (over z).
Axes of the slice: x: 4, y: 4, z: 4, core: 2. Of those that a mesh axis runs over, the one named last changes fastest.
Arguments:
- particles: float32 [6, 262144], P(None, ('slab', 'lane')), as said below
- pair_list: int32 [32, 32768], P(None, ('slab', 'lane')), may hold values from 0 to 2303, as said below
- pair_count: int32 [32768], P(('slab', 'lane')), may hold values from 2 to 32, as said below
Outputs:
- short_forces: float32 [3, 262144], P(None, ('slab', 'lane'))
- long_forces: float32 [3, 262144], P(None, ('slab', 'lane'))
Inputs may be any that keep to these rules, and one draw needn't show every extreme that they name: `particles`: column a*256+c of a device's block is atom a = 4*ax+2*ay+az of cluster c = (cx*4+cy)*16+cz; its position lies within 0.03 nm of lattice site ((2cx+ax+0.5)*0.3, (2cy+ay+0.5)*0.3, (2cz+az+0.5)*0.12*256/32) in the brick's own frame; charges lie in -1.5 to 1.5, row 4 in 0.003 to 0.01, row 5 in 3e-5 to 1e-4. `pair_list`: entry j = (3*(bx+1)+(by+1))*256+c' names cluster c' of the brick bx slab steps and by lane steps away (periodic); it lies within two cluster steps of the listing cluster along x and y and one along z (periodic in z); the entries of a column are distinct. Slots 0 to pair_count-1 of a cluster's column are used; loads differ widely between bricks.
All inputs are finite; a program needn't handle non-finite values.
Results may differ from a plain program's by a relative error of at most 0.0003.
Values sent between devices are 32-bit elements; how exact they have to be, the bound alone decides.
A program may use at most 192 MiB of HBM per device.

v0:
```python
import math

import jax
import jax.numpy as jnp
from jax import lax
from jax.sharding import PartitionSpec as P

LAT_X = 8
LAT_Y = 8
CELLS_X = 15
CELLS_Y = 40
GZ = 256


SPACING = 0.3
CELL_Z = 0.12
CUTOFF = 1.2
EWALD_BETA = 2.6
slot_block = 16
HIGHEST = lax.Precision.HIGHEST


def padded(block, sides, width):
    for axis, dim in sides:
        count = lax.axis_size(axis)
        forward = [(i, i + 1) for i in range(count - 1)]
        forward.append((count - 1, 0))
        backward = [(target, source) for source, target in forward]
        low = lax.ppermute(
            lax.slice_in_dim(block, block.shape[dim] - width, None, axis=dim), axis, forward
        )
        high = lax.ppermute(lax.slice_in_dim(block, 0, width, axis=dim), axis, backward)
        block = jnp.concatenate([low, block, high], axis=dim)
    return block


def spline_value(argument):
    magnitude = jnp.abs(argument)
    inner = 2.0 / 3.0 - magnitude * magnitude + 0.5 * magnitude * magnitude * magnitude
    outer = jnp.maximum(2.0 - magnitude, 0.0) ** 3 / 6.0
    return jnp.where(magnitude < 1.0, inner, outer)


def spline_slope(argument):
    magnitude = jnp.abs(argument)
    inner = argument * (1.5 * magnitude - 2.0)
    outer = -jnp.sign(argument) * 0.5 * jnp.maximum(2.0 - magnitude, 0.0) ** 2
    return jnp.where(magnitude < 1.0, inner, outer)


def stencil(coordinate):
    lowest = jnp.floor(coordinate) - 1.0
    cell_pos = lowest[None, :] + jnp.arange(4).astype(coordinate.dtype)[:, None]
    offset = coordinate[None, :] - cell_pos
    return (cell_pos.astype(jnp.int32), spline_value(offset), spline_slope(offset))


def signed_wave(wave_index, length_count):
    return jnp.where(wave_index < (length_count + 1) // 2, wave_index, wave_index - length_count)


def spline_modulus(wave_index, length_count):
    angle = wave_index.astype(jnp.float32) * (2.0 * math.pi / length_count)
    return 1.0 / (2.0 / 3.0 + jnp.cos(angle) / 3.0) ** 2


def influence(wave_x, wave_y, wave_z, count_x, count_y, length_x, length_y):
    length_z = GZ * CELL_Z
    freq_x = signed_wave(wave_x, count_x).astype(jnp.float32) / length_x
    freq_y = signed_wave(wave_y, count_y).astype(jnp.float32) / length_y
    freq_z = signed_wave(wave_z, GZ).astype(jnp.float32) / length_z
    norm_sq = freq_x * freq_x + freq_y * freq_y + freq_z * freq_z
    safe_sq = jnp.where(norm_sq > 0, norm_sq, 1.0)
    moduli = (
        spline_modulus(wave_x, count_x)
        * spline_modulus(wave_y, count_y)
        * spline_modulus(wave_z, GZ)
    )
    value = (
        jnp.exp(-((math.pi / EWALD_BETA) ** 2) * safe_sq)
        * moduli
        / (math.pi * length_x * length_y * length_z * safe_sq)
    )
    return jnp.where(norm_sq > 0, value, 0.0)


def dft_table(length_count):
    position = jnp.arange(length_count, dtype=jnp.int32)
    phase = position[:, None] * position[None, :] % length_count
    angle = phase.astype(jnp.float32) * (2.0 * math.pi / length_count)
    return (jnp.cos(angle), jnp.sin(angle))


def rotate(real_part, imag_part, cosine, sine_table, pattern, direction):
    real_cos = jnp.einsum(pattern, real_part, cosine, precision=HIGHEST)
    real_sin = jnp.einsum(pattern, real_part, sine_table, precision=HIGHEST)
    imag_cos = jnp.einsum(pattern, imag_part, cosine, precision=HIGHEST)
    imag_sin = jnp.einsum(pattern, imag_part, sine_table, precision=HIGHEST)
    return (real_cos + direction * imag_sin, imag_cos - direction * real_sin)


def fold_rims(rimmed, axis_dim, inner):
    core = lax.slice_in_dim(rimmed, 4, inner + 4, axis=axis_dim)
    lower_rim = lax.slice_in_dim(rimmed, 0, 2, axis=axis_dim)
    upper_rim = lax.slice_in_dim(rimmed, inner + 6, inner + 8, axis=axis_dim)
    low_widths = [(0, 0)] * rimmed.ndim
    high_widths = [(0, 0)] * rimmed.ndim
    low_widths[axis_dim] = (0, inner - 2)
    high_widths[axis_dim] = (inner - 2, 0)
    return core + jnp.pad(lower_rim, low_widths) + jnp.pad(upper_rim, high_widths)


def pair_terms(owned, nearby, slot_rows, live_mask, center):
    joined = jnp.take(nearby, slot_rows, axis=2)
    own_side = owned[:, None, None, :, :]
    far_side = joined[:, :, :, None, :]
    diff_x = own_side[0] - far_side[0]
    diff_y = own_side[1] - far_side[1]
    diff_z = own_side[2] - far_side[2]
    box_z = GZ * CELL_Z
    diff_z = diff_z - box_z * jnp.floor(diff_z / box_z + 0.5)
    atom_ids = jnp.arange(8)
    same_atom = (slot_rows == center[None, :])[None, :, None, :] & (
        atom_ids[:, None] == atom_ids[None, :]
    )[:, None, :, None]
    keep = live_mask[None, :, None, :] & jnp.logical_not(same_atom)
    dist_sq = diff_x * diff_x + diff_y * diff_y + diff_z * diff_z
    safe_sq = jnp.where(keep, dist_sq, 1.0)
    inverse = 1.0 / safe_sq
    distance = jnp.sqrt(safe_sq)
    inverse_six = inverse * inverse * inverse
    dispersion = (
        12.0 * own_side[5] * far_side[5] * inverse_six - 6.0 * own_side[4] * far_side[4]
    ) * inverse_six
    coulomb = (
        own_side[3]
        * far_side[3]
        * (
            jax.scipy.special.erfc(EWALD_BETA * distance) / distance
            + 2.0 * EWALD_BETA / math.sqrt(math.pi) * jnp.exp(-(EWALD_BETA**2) * safe_sq)
        )
    )
    switch = jnp.maximum(1.0 - safe_sq / (CUTOFF * CUTOFF), 0.0) ** 2
    scalar = jnp.where(keep, (dispersion + coulomb) * inverse * switch, 0.0)
    return jnp.stack(
        [
            jnp.sum(scalar * diff_x, axis=(0, 1)),
            jnp.sum(scalar * diff_y, axis=(0, 1)),
            jnp.sum(scalar * diff_z, axis=(0, 1)),
        ]
    )


def shards(particles, pair_list, pair_count):
    atom_dev = particles.shape[1]
    clusters = atom_dev // 8
    num_slab = lax.axis_size("slab")
    num_lane = lax.axis_size("lane")
    slab_at = lax.axis_index("slab")
    lane_at = lax.axis_index("lane")
    brick_x = LAT_X * SPACING
    brick_y = LAT_Y * SPACING
    cell_x = brick_x / CELLS_X
    cell_y = brick_y / CELLS_Y
    grid_x = CELLS_X * num_slab
    grid_y = CELLS_Y * num_lane
    planes = GZ // (num_slab * num_lane)
    beside_all = padded(particles.reshape(1, 1, 6, atom_dev), (("slab", 0), ("lane", 1)), 1)
    shift_x = (jnp.arange(3) - 1).astype(jnp.float32)[:, None, None, None] * brick_x
    shift_y = (jnp.arange(3) - 1).astype(jnp.float32)[None, :, None, None] * brick_y
    placed = jnp.concatenate(
        [beside_all[:, :, 0:1] + shift_x, beside_all[:, :, 1:2] + shift_y, beside_all[:, :, 2:]],
        axis=2,
    )
    nearby = placed.reshape(9, 6, 8, clusters).transpose(1, 2, 0, 3).reshape(6, 8, 9 * clusters)
    owned = particles.reshape(6, 8, clusters)
    center = 4 * clusters + jnp.arange(clusters, dtype=jnp.int32)

    def block_step(block_id, running):
        first_slot = (block_id * slot_block).astype(jnp.int32)
        slot_rows = lax.dynamic_slice_in_dim(pair_list, first_slot, slot_block, 0)
        live_mask = (first_slot + jnp.arange(slot_block, dtype=jnp.int32))[:, None] < pair_count[
            None, :
        ]
        return running + pair_terms(owned, nearby, slot_rows, live_mask, center)

    block_total = pair_list.shape[0] // slot_block
    short_block = lax.fori_loop(
        0, block_total, block_step, jnp.zeros((3, 8, clusters), jnp.float32)
    )
    short_forces = short_block.reshape(3, atom_dev)
    charge = particles[3]
    index_x, weight_x, slope_x = stencil(particles[0] / cell_x)
    index_y, weight_y, slope_y = stencil(particles[1] / cell_y)
    index_z, weight_z, slope_z = stencil(particles[2] / CELL_Z)
    wide_x = CELLS_X + 4
    wide_y = CELLS_Y + 4
    padded_index = (
        ((index_z % GZ)[None, None, :, :] * wide_x + index_x[:, None, None, :] + 2) * wide_y
        + index_y[None, :, None, :]
        + 2
    )
    own_weight = (
        charge
        * weight_x[:, None, None, :]
        * weight_y[None, :, None, :]
        * weight_z[None, None, :, :]
    )
    widened = (
        jnp.zeros(GZ * wide_x * wide_y, jnp.float32)
        .at[padded_index.reshape(-1)]
        .add(own_weight.reshape(-1))
        .reshape(GZ, wide_x, wide_y)
    )
    rimmed = padded(widened, (("slab", 1), ("lane", 2)), 2)
    charge_grid = fold_rims(fold_rims(rimmed, 1, CELLS_X), 2, CELLS_Y)
    cos_z, sin_z = dft_table(GZ)
    cos_x, sin_x = dft_table(grid_x)
    cos_y, sin_y = dft_table(grid_y)
    real_z = jnp.einsum("zxy,zk->kxy", charge_grid, cos_z, precision=HIGHEST)
    imag_z = -jnp.einsum("zxy,zk->kxy", charge_grid, sin_z, precision=HIGHEST)
    spectrum = jnp.stack([real_z, imag_z])
    received = lax.all_to_all(
        spectrum.reshape(2, GZ, CELLS_X * CELLS_Y),
        ("slab", "lane"),
        split_axis=1,
        concat_axis=2,
        tiled=True,
    )
    middle = (
        received.reshape(2, planes, num_slab, num_lane, CELLS_X, CELLS_Y)
        .transpose(0, 1, 2, 4, 3, 5)
        .reshape(2, planes, grid_x, grid_y)
    )
    first_plane = (slab_at * num_lane + lane_at) * planes
    real_part, imag_part = rotate(middle[0], middle[1], cos_x, sin_x, "zxy,xk->zky", 1.0)
    real_part, imag_part = rotate(real_part, imag_part, cos_y, sin_y, "zxy,yk->zxk", 1.0)
    wave_z = first_plane + jnp.arange(planes, dtype=jnp.int32)
    kernel = influence(
        jnp.arange(grid_x, dtype=jnp.int32)[None, :, None],
        jnp.arange(grid_y, dtype=jnp.int32)[None, None, :],
        wave_z[:, None, None],
        grid_x,
        grid_y,
        brick_x * num_slab,
        brick_y * num_lane,
    )
    real_part = real_part * kernel
    imag_part = imag_part * kernel
    real_part, imag_part = rotate(real_part, imag_part, cos_y, sin_y, "zxy,yk->zxk", -1.0)
    real_part, imag_part = rotate(real_part, imag_part, cos_x, sin_x, "zxy,xk->zky", -1.0)
    convolved = jnp.stack([real_part, imag_part])
    outgoing = (
        convolved.reshape(2, planes, num_slab, CELLS_X, num_lane, CELLS_Y)
        .transpose(0, 1, 2, 4, 3, 5)
        .reshape(2, planes, num_slab * num_lane * CELLS_X * CELLS_Y)
    )
    returned = lax.all_to_all(
        outgoing, ("slab", "lane"), split_axis=2, concat_axis=1, tiled=True
    ).reshape(2, GZ, CELLS_X, CELLS_Y)
    potential = jnp.einsum("kxy,kz->zxy", returned[0], cos_z, precision=HIGHEST) - jnp.einsum(
        "kxy,kz->zxy", returned[1], sin_z, precision=HIGHEST
    )
    widened_potential = padded(potential, (("slab", 1), ("lane", 2)), 2)
    sampled = widened_potential.reshape(-1)[padded_index]
    along_x = jnp.sum(
        sampled
        * (slope_x / cell_x)[:, None, None, :]
        * weight_y[None, :, None, :]
        * weight_z[None, None, :, :],
        axis=(0, 1, 2),
    )
    along_y = jnp.sum(
        sampled
        * weight_x[:, None, None, :]
        * (slope_y / cell_y)[None, :, None, :]
        * weight_z[None, None, :, :],
        axis=(0, 1, 2),
    )
    along_z = jnp.sum(
        sampled
        * weight_x[:, None, None, :]
        * weight_y[None, :, None, :]
        * (slope_z / CELL_Z)[None, None, :, :],
        axis=(0, 1, 2),
    )
    long_forces = -charge * jnp.stack([along_x, along_y, along_z])
    return (short_forces, long_forces)


def solution(mesh):
    in_specs = (P(None, ("slab", "lane")), P(None, ("slab", "lane")), P(("slab", "lane")))
    out_specs = (P(None, ("slab", "lane")), P(None, ("slab", "lane")))
    return jax.shard_map(shards, mesh=mesh, in_specs=in_specs, out_specs=out_specs, check_vma=False)
```

profile of v0, /device:TPU:5, one launch (start us, length us, event | category | flops | bytes accessed | tf_op | source)
XLA Modules:
  0.0 2268.3 jit_solution(6209090542944302597)
XLA Ops:
  7.9 683.0 %scatter_custom_fusion = f32[214016]{0:T(1024)} fusion(s32[131072]{0:T(1024)S(1)} %bitcast.214, f32[131072]{0:T(1024)S(1)} %bitcast.215, f32[]{:T(128)} %constant.418.clone.1), kind=kCustom, calls=%fused_computation.154 | custom fusion | flops 131072 | bytes 856068 | tf_op jit(solution)/shard_map/scatter-add | solution.py:212
  704.5 3.6 fusion.298
  729.1 13.1 all-to-all-start
  749.2 12.8 all-to-all-done
  762.1 4.1 reshape.859
  774.4 7.1 fusion.50
  781.5 5.9 fusion.44
  792.2 5.8 fusion.42
  798.0 5.6 fusion.52
  814.0 5.8 fusion.40
  819.8 6.0 fusion.46
  827.2 5.6 fusion.48
  832.9 6.4 fusion.38
  846.6 4.6 maximum_bitcast_fusion
  851.2 78.8 %copy.99 = f32[2,2,32,4,15,40]{1,0,5,4,3,2:T(2,128)} copy(f32[2,2,32,4,15,40]{5,3,4,2,1,0:T(4,128)} %maximum_bitcast_fusion) | data formatting | bytes 2457600 | tf_op jit(solution)/shard_map/reshape | solution.py:256
  930.0 115.6 %reshape.953 = f32[128,1,2400]{2,1,0:T(1,128)} reshape(f32[76800,2,2]{2,1,0:T(2,128)} %bitcast.121) | data formatting | bytes 2457600
  1045.6 6.9 all-to-all-start.1
  1054.2 17.3 all-to-all-done.1
  1075.6 151.0 %reshape.954 = f32[76800,2,2]{2,1,0:T(2,128)} reshape(f32[128,2400]{1,0:T(8,128)S(1)} %reduce.24) | data formatting | bytes 2457600
  1226.6 64.9 %copy.100 = f32[2,2,128,600]{3,2,1,0:T(8,128)S(1)} copy(f32[2,2,128,600]{1,0,3,2:T(2,128)} %bitcast.53) | data formatting | bytes 2457600 | tf_op jit(solution)/shard_map/all_to_all | solution.py:258
  1297.8 3.6 fusion.138
  1310.3 5.3 copy.76
  1319.0 215.5 %while.14 = (s32[]{:T(128)}, f32[3,8,256]{2,1,0:T(8,128)S(1)}, s32[256]{0:T(256)S(1)}, s32[32,256]{1,0:T(8,128)S(1)}, f32[6,2048]{1,0:T(8,128)S(1)}, /*index=5*/...) while((s32[]{:T(128)}, f32[3,8,256]{2,1,0:T(8,128)S(1)}, s32[256]{0:T(256)S(1)}, ...), condition=%wide.region_4.5_spmd.clone, body=%wide.region_0.4_spmd.clone.sunk | while | flops 28055892 | bytes 7581097 | solution.py:188
  1319.4 34.7 %gather_fusion = f32[4096,6,8]{2,1,0:T(8,128)} fusion(f32[6,8,2304]{1,0,2:T(8,128)} %get-tuple-element.324, s32[4096]{0:T(1024)S(1)} %broadcast_clamp_fusion.3), kind=kCustom, calls=%fused_computation.clone.clone.1 | custom fusion | bytes 1589248 | tf_op jit(solution)/shard_map/while/body/eval_jaxpr/jit(_take)/gather | solution.py:114
  1354.2 11.9 select_bitcast_fusion.2
  1366.1 43.3 %fusion.322 = (f32[1,8,16,256]{1,0,3,2:T(1,128)S(1)}, f32[1,8,16,256]{1,0,3,2:T(1,128)}, f32[1,8,16,256]{1,0,3,2:T(1,128)}, f32[1,8,16,256]{1,0,3,2:T(1,128)}, f...) fusion(f32[6,8,16,256]{1,0,3,2:T(8,128)} %select_bitcast_fusion.2), kind=kLoop, calls=%fused_computation.382.clone.1 | loop fusion | bytes 1572864 | tf_op jit(solution)/shard_map/while/body/eval_jaxpr/slice | solution.py:133
  1421.8 5.1 fusion.323
  1427.0 34.7 %gather_fusion = f32[4096,6,8]{2,1,0:T(8,128)} fusion(f32[6,8,2304]{1,0,2:T(8,128)} %get-tuple-element.324, s32[4096]{0:T(1024)S(1)} %broadcast_clamp_fusion.3), kind=kCustom, calls=%fused_computation.clone.clone.1 | custom fusion | bytes 1589248 | tf_op jit(solution)/shard_map/while/body/eval_jaxpr/jit(_take)/gather | solution.py:114
  1461.8 11.9 select_bitcast_fusion.2
  1473.7 43.3 %fusion.322 = (f32[1,8,16,256]{1,0,3,2:T(1,128)S(1)}, f32[1,8,16,256]{1,0,3,2:T(1,128)}, f32[1,8,16,256]{1,0,3,2:T(1,128)}, f32[1,8,16,256]{1,0,3,2:T(1,128)}, f...) fusion(f32[6,8,16,256]{1,0,3,2:T(8,128)} %select_bitcast_fusion.2), kind=kLoop, calls=%fused_computation.382.clone.1 | loop fusion | bytes 1572864 | tf_op jit(solution)/shard_map/while/body/eval_jaxpr/slice | solution.py:133
  1529.4 5.1 fusion.323
  1541.6 724.9 %gather_fusion.1 = f32[131072]{0:T(1024)S(1)} fusion(f32[214016]{0:T(1024)S(1)} %reshape.861, s32[131072]{0:T(1024)S(1)} %copy-done.4), kind=kCustom, calls=%fused_computation.1 | custom fusion | bytes 1572864 | tf_op jit(solution)/shard_map/gather | solution.py:265
  (211 shorter events, 138.0 us)
Async XLA Ops:
  0.6 743.7 %collective-permute-start = (f32[1,1,6,2048]{3,2,1,0:T(8,128)}, f32[1,1,6,2048]{3,2,1,0:T(8,128)S(1)}, u32[]{:S(2)}, u32[]{:S(2)}) collective-permute-start(f32[1,1,6,2048]{3,2,1,0:T(8,128)} %bitcast.178), channel_id=1, source_target_pairs={{0,4},{4,8},{8,12},{12,16},{16,20},{20,24},{24,28},{28,32},{32,36}... | collective-permute-start | bytes 147464 | tf_op jit(solution)/shard_map/ppermute | solution.py:29
  2.6 741.8 %collective-permute-start.1 = (f32[1,1,6,2048]{3,2,1,0:T(8,128)}, f32[1,1,6,2048]{3,2,1,0:T(8,128)S(1)}, u32[]{:S(2)}, u32[]{:S(2)}) collective-permute-start(f32[1,1,6,2048]{3,2,1,0:T(8,128)} %bitcast.179), channel_id=1, source_target_pairs={{4,0},{8,4},{12,8},{16,12},{20,16},{24,20},{28,24},{32,28},{36,32}... | collective-permute-start | bytes 147464 | tf_op jit(solution)/shard_map/ppermute | solution.py:32
  693.8 5.3 copy-start
  694.0 5.1 collective-permute-start.4
  695.8 6.1 collective-permute-start.5
  711.1 8.9 collective-permute-start.6
  715.7 4.3 collective-permute-start.7
  729.1 15.9 copy-start.2
  729.1 32.9 %all-to-all-start = ((f32[2,256,600]{2,0,1:T(2,128)}), f32[2,256,600]{2,0,1:T(2,128)S(1)}, u32[]{:S(2)}, u32[]{:S(2)}) async-start(f32[2,256,600]{2,0,1:T(2,128)} %pad_maximum_fusion.1), calls=%async_computation | async-start | bytes 2621440 | tf_op jit(solution)/shard_map/all_to_all | solution.py:223
  745.7 307.7 %collective-permute-start.2 = (f32[3,1,6,2048]{3,2,1,0:T(8,128)}, f32[3,1,6,2048]{3,2,1,0:T(8,128)S(1)}, u32[]{:S(2)}, u32[]{:S(2)}) collective-permute-start(f32[3,1,6,2048]{3,2,1,0:T(8,128)} %pad_maximum_fusion.4), channel_id=1, source_target_pairs={{0,1},{1,2},{2,3},{3,0},{4,5},{5,6},{6,7},{7,4},{8,9},{9,10},{10,1... | collective-permute-start | bytes 442376 | tf_op jit(solution)/shard_map/ppermute | solution.py:29
  747.0 306.4 %collective-permute-start.3 = (f32[3,1,6,2048]{3,2,1,0:T(8,128)}, f32[3,1,6,2048]{3,2,1,0:T(8,128)S(1)}, u32[]{:S(2)}, u32[]{:S(2)}) collective-permute-start(f32[3,1,6,2048]{3,2,1,0:T(8,128)} %pad_maximum_fusion.4), channel_id=1, source_target_pairs={{1,0},{2,1},{3,2},{0,3},{5,4},{6,5},{7,6},{4,7},{9,8},{10,9},{11,1... | collective-permute-start | bytes 442376 | tf_op jit(solution)/shard_map/ppermute | solution.py:32
  774.4 7.1 copy-start.6
  792.2 11.4 copy-start.7
  798.0 7.1 copy-start.8
  1045.6 6.9 copy-start.3
  1045.6 7.9 copy-start.10
  1045.6 7.9 copy-start.12
  1045.6 26.0 %all-to-all-start.1 = ((f32[128,1,2400]{2,1,0:T(1,128)}), f32[128,1,2400]{2,1,0:T(1,128)S(1)}, u32[]{:S(2)}, u32[]{:S(2)}) async-start(f32[128,1,2400]{2,1,0:T(1,128)} %reshape.953), calls=%async_computation.1 | async-start | bytes 2490368 | tf_op jit(solution)/shard_map/all_to_all | solution.py:258
  1306.5 3.5 copy-start.17
  1309.3 6.3 collective-permute-start.8
  1309.8 5.8 collective-permute-start.9
  1310.3 8.7 copy-start.5
  1310.3 8.7 copy-start.27
  1316.3 218.8 %collective-permute-start.10 = (f32[256,19,2]{0,2,1:T(2,128)}, f32[256,19,2]{0,2,1:T(2,128)}, u32[]{:S(2)}, u32[]{:S(2)}) collective-permute-start(f32[256,19,2]{0,2,1:T(2,128)} %get-tuple-element.191), channel_id=1, source_target_pairs={{0,1},{1,2},{2,3},{3,0},{4,5},{5,6},{6,7},{7,4},{8,9},{9,10},{10,1... | collective-permute-start | bytes 116744 | tf_op jit(solution)/shard_map/ppermute | solution.py:29
  1316.8 218.3 %collective-permute-start.11 = (f32[256,19,2]{0,2,1:T(2,128)}, f32[256,19,2]{0,2,1:T(2,128)}, u32[]{:S(2)}, u32[]{:S(2)}) collective-permute-start(f32[256,19,2]{0,2,1:T(2,128)} %get-tuple-element.192), channel_id=1, source_target_pairs={{1,0},{2,1},{3,2},{0,3},{5,4},{6,5},{7,6},{4,7},{9,8},{10,9},{11,1... | collective-permute-start | bytes 116744 | tf_op jit(solution)/shard_map/ppermute | solution.py:32
  1541.5 725.1 %copy-start.19 = (f32[4,2048]{1,0:T(4,128)S(1)}, f32[4,2048]{1,0:T(4,128)}, u32[]{:S(2)}) copy-start(f32[4,2048]{1,0:T(4,128)} %copy-done.18) | copy-start | bytes 98308
  1541.5 725.1 %copy-start.21 = (f32[4,2048]{1,0:T(4,128)S(1)}, f32[4,2048]{1,0:T(4,128)}, u32[]{:S(2)}) copy-start(f32[4,2048]{1,0:T(4,128)} %copy-done.20) | copy-start | bytes 98308
  1541.5 725.1 %copy-start.22 = (f32[4,2048]{1,0:T(4,128)S(1)}, f32[4,2048]{1,0:T(4,128)}, u32[]{:S(2)}) copy-start(f32[4,2048]{1,0:T(4,128)} %get-tuple-element.207) | copy-start | bytes 98308
  1541.5 725.1 %copy-start.23 = (f32[4,2048]{1,0:T(4,128)S(1)}, f32[4,2048]{1,0:T(4,128)}, u32[]{:S(2)}) copy-start(f32[4,2048]{1,0:T(4,128)} %get-tuple-element.217) | copy-start | bytes 98308
  1541.5 725.1 %copy-start.24 = (f32[4,2048]{1,0:T(4,128)S(1)}, f32[4,2048]{1,0:T(4,128)}, u32[]{:S(2)}) copy-start(f32[4,2048]{1,0:T(4,128)} %get-tuple-element.219) | copy-start | bytes 98308
  1541.5 725.1 %copy-start.25 = (f32[4,2048]{1,0:T(4,128)S(1)}, f32[4,2048]{1,0:T(4,128)}, u32[]{:S(2)}) copy-start(f32[4,2048]{1,0:T(4,128)} %get-tuple-element.221) | copy-start | bytes 98308
  1541.6 725.7 %copy-start.26 = (f32[1,2048]{1,0:T(1,128)S(1)}, f32[1,2048]{1,0:T(1,128)}, u32[]{:S(2)}) copy-start(f32[1,2048]{1,0:T(1,128)} %get-tuple-element.199) | copy-start | bytes 24580
  (12 other events, 24.6 us)
where the time goes:
time: 2290 us; the launch traced here: 2270 us
  local copies, waits for them, and re-layouts  1380 us (60%)
  other arithmetic  747 us (33%)
  matrix products  68.5 us (3%)
  starting transfers between devices  35.5 us (2%)
  waiting for transfers between devices  35.2 us (2%)
    gather x2, local copies, waits for them, and re-layouts, shards(): sampled = widened_potential.reshape(-1)[padded_index]  725 us
    scatter-add x1, other arithmetic, shards(): widened = jnp.zeros(GZ * wide_x * wide_y, jnp.float32).at[padded_index.re...  683 us
    unnamed x65, local copies, waits for them, and re-layouts  269 us
    slice x2, local copies, waits for them, and re-layouts, pair_terms(): far_side[5]  86.7 us
    reshape x1, local copies, waits for them, and re-layouts, shards(): outgoing = convolved.reshape(2, planes, num_slab, CELLS_X, num_lane, CELL...  78.8 us
    gather x2, local copies, waits for them, and re-layouts, pair_terms(): joined = jnp.take(nearby, slot_rows, axis=2)  69.5 us
    all_to_all x2, local copies, waits for them, and re-layouts, shards(): lax.all_to_all(outgoing, ('slab', 'lane'), split_axis=2, concat_axis=1, t...  65.4 us
    unnamed x12, matrix products  56.8 us
  transfers between devices with their start and end apart: 14, of which 4 were waited for; matrix products, arithmetic and copies ran while one was open for 54% of the time, Pallas kernels for 0%

commit v1 on v0

v1 whole, which is shorter than its diff:
```python
import functools
import math

import jax
import jax.numpy as jnp
import numpy as np
from jax import lax
from jax.experimental import pallas as pl
from jax.experimental.pallas import tpu as pltpu
from jax.sharding import PartitionSpec as P

SPACING = 0.3
CELL_Z = 0.12
CUTOFF = 1.2
EWALD_BETA = 2.6
CELLS_X = 15
CELLS_Y = 40
GZ = 256
N_SLAB = 32
N_LANE = 4
GX = CELLS_X * N_SLAB
GY = CELLS_Y * N_LANE
BRICK = 8 * SPACING
HX = BRICK / CELLS_X
HY = BRICK / CELLS_Y
BOX_Z = GZ * CELL_Z
SITE_Z = BOX_Z / 32
DEVICES = N_SLAB * N_LANE
WIN_X = 18
ERFCX = (
    0.2256758607181025,
    0.22566977328080512,
    0.2078385838830704,
    0.1685781716404984,
    0.1412773409832938,
    -0.005255409952977477,
    0.1686438579877198,
    -0.18261534673649704,
    0.050187288302216415,
)
f32 = jnp.float32
VMEM = pl.BlockSpec(memory_space=pltpu.VMEM)


def x_window(site):
    low = 1.875 * (site + 0.5) - 0.1875
    high = 1.875 * (site + 0.5) + 0.1875
    first = math.floor(low) - 1
    last = math.ceil(high) + 1
    return [cell for cell in range(first, last + 1) if cell - 2 < high - 1e-6 and cell + 2 > low + 1e-6]


X_WINDOWS = [x_window(site) for site in range(8)]


def dft_basis(count):
    half = count // 2
    waves = np.concatenate([np.arange(half + 1), np.arange(1, half)])
    is_sine = np.arange(count) > half
    phase = np.outer(waves, np.arange(count)) % count
    angle = phase * (2.0 * np.pi / count)
    return waves, np.where(is_sine[:, None], np.sin(angle), np.cos(angle))


def wave_factor(waves, count, length):
    freq_sq = (waves / length) ** 2
    modulus = (2.0 / 3.0 + np.cos(2.0 * np.pi * waves / count) / 3.0) ** -2
    twice = np.where((waves == 0) | (2 * waves == count), 1.0, 2.0)
    return np.exp(-((np.pi / EWALD_BETA) ** 2) * freq_sq) * modulus * twice, freq_sq


def tables():
    waves_x, basis_x = dft_basis(GX)
    waves_y, basis_y = dft_basis(GY)
    cells = (15 * np.arange(N_SLAB)[None, :] + np.arange(WIN_X)[:, None] - 1) % GX
    forward_x = basis_x[:, cells.reshape(-1)]
    lane, cy, jy, ay = np.meshgrid(np.arange(4), np.arange(4), np.arange(4), np.arange(2), indexing="ij")
    rows = 40 * lane + 5 * (2 * cy + ay) + jy + 1
    forward_y = basis_y[:, rows.reshape(-1)].T
    kz = np.concatenate([np.arange(128), [128], np.arange(1, 128)])
    sine = np.arange(256) > 128
    jz, az, cy, cz = np.meshgrid(np.arange(5), np.arange(2), np.arange(4), np.arange(16), indexing="ij")
    cell = (8 * (2 * cz + az) + jz + 2).reshape(-1)
    angle = (np.outer(kz, cell) % GZ) * (2.0 * np.pi / GZ)
    basis_z = np.where(sine[:, None], np.sin(angle), np.cos(angle))
    gain_x, sq_x = wave_factor(waves_x, GX, BRICK * N_SLAB)
    gain_y, sq_y = wave_factor(waves_y, GY, BRICK * N_LANE)
    gain_z, sq_z = wave_factor(kz, GZ, BOX_Z)
    gain_z = gain_z / (np.pi * BRICK * N_SLAB * BRICK * N_LANE * BOX_Z)
    column = np.stack([gain_x, sq_x], axis=1)
    row = np.stack([gain_y, sq_y])
    plane = np.stack([gain_z.reshape(2, 128), sq_z.reshape(2, 128)], axis=-1).transpose(1, 0, 2)
    return {
        "z": basis_z.astype(np.float32),
        "x": forward_x.astype(np.float32),
        "xt": np.ascontiguousarray(forward_x.T).astype(np.float32),
        "y": forward_y.astype(np.float32),
        "yt": np.ascontiguousarray(forward_y.T).astype(np.float32),
        "col": column.astype(np.float32),
        "row": row.astype(np.float32),
        "plane": plane.astype(np.float32),
    }


def lanes(shape=(8, 128)):
    return lax.broadcasted_iota(jnp.int32, shape, 1)


def sublanes(shape=(8, 128)):
    return lax.broadcasted_iota(jnp.int32, shape, 0)


def ahead(value, step):
    return pltpu.roll(value, (-step) % 128, axis=1)


def matmul(left, right, transposed=False):
    dims = (((1,), (1,)), ((), ())) if transposed else (((1,), (0,)), ((), ()))
    return lax.dot_general(
        left, right, dims, precision=lax.Precision.HIGHEST, preferred_element_type=f32
    )


def spline(offset, slope):
    size = jnp.abs(offset)
    outer = jnp.maximum(2.0 - size, 0.0)
    outer_sq = outer * outer
    near = size < 1.0
    value = jnp.where(near, 2.0 / 3.0 + size * size * (0.5 * size - 1.0), outer_sq * outer * (1.0 / 6.0))
    if not slope:
        return value
    half = 0.5 * outer_sq
    derivative = jnp.where(near, offset * (1.5 * size - 2.0), jnp.where(offset < 0.0, half, -half))
    return value, derivative


def pick_site(z_ref, site, attr):
    even = jnp.broadcast_to(z_ref[0, site, attr : attr + 1, :], (8, 128))
    odd = jnp.broadcast_to(z_ref[1, site, attr : attr + 1, :], (8, 128))
    return jnp.where(sublanes() % 2 == 0, even, odd)


def site_offsets(z_ref, site):
    lane = lanes()
    sub = sublanes()
    along_x = (pick_site(z_ref, site, 0) - (site + 0.5) * SPACING) * (1.0 / HX)
    site_y = (2 * ((lane >> 4) & 3) + (sub & 1)).astype(f32)
    along_y = (pick_site(z_ref, site, 1) - (site_y + 0.5) * SPACING) * (1.0 / HY)
    site_z = (2 * (lane & 15) + (lane >> 6)).astype(f32)
    along_z = (pick_site(z_ref, site, 2) - (site_z + 0.5) * SITE_Z) * (1.0 / CELL_Z)
    along_y = along_y + (1.5 - (sub >> 1).astype(f32))
    return along_x, along_y, along_z, pick_site(z_ref, site, 3)


def pack_particles(part_ref, z_ref):
    lane = lanes((6, 128))
    low = lane < 64
    for ax in range(2):
        for ay in range(2):
            for pair in range(2):
                first = ((ax * 2 + ay) * 2) * 256 + pair * 128
                v0 = part_ref[:, first : first + 128]
                v1 = part_ref[:, first + 256 : first + 384]
                x = 4 * pair + ax
                z_ref[ay, x, 0:6, :] = jnp.where(low, v0, ahead(v1, 64))
                z_ref[ay, x + 2, 0:6, :] = jnp.where(low, ahead(v0, 64), v1)
    for x in range(8):
        even = z_ref[0, x, 0:6, :]
        odd = z_ref[1, x, 0:6, :]
        upper = ((lane >> 5) & 1) == 1
        z_ref[2, x, 0:6, :] = jnp.where(upper, even, ahead(odd, 32))
        z_ref[3, x, 0:6, :] = jnp.where(upper, ahead(odd, -32), even)


def unpack_forces(o_ref, out_ref):
    low = lanes() < 64
    for ax in range(2):
        for ay in range(2):
            for pair in range(2):
                first = ((ax * 2 + ay) * 2) * 256 + pair * 128
                x = 4 * pair + ax
                even = o_ref[ay, x]
                odd = o_ref[ay, x + 2]
                out_ref[:, first : first + 128] = jnp.where(low, even, ahead(odd, 64))[0:3]
                out_ref[:, first + 256 : first + 384] = jnp.where(low, ahead(even, 64), odd)[0:3]


def spread_charges(z_ref, ball_ref):
    lane_cy = (lanes() >> 4) & 3
    grid = {}

    def flush(cell):
        column = cell + 1
        for jz in range(5):
            value = grid.pop((cell, jz))
            for cy in range(4):
                row = (column * 4 + cy) * 8
                ball_ref[row : row + 8, jz * 128 : (jz + 1) * 128] = jnp.where(lane_cy == cy, value, 0.0)

    for site in range(8):
        along_x, along_y, along_z, charge = site_offsets(z_ref, site)
        charge_y = charge * spline(along_y, False)
        charge_yz = [charge_y * spline(along_z + (2.0 - jz), False) for jz in range(5)]
        for cell in X_WINDOWS[site]:
            weight = spline(along_x + (1.875 * (site + 0.5) - cell), False)
            for jz in range(5):
                term = weight * charge_yz[jz]
                key = (cell, jz)
                grid[key] = grid[key] + term if key in grid else term
        coming = X_WINDOWS[site + 1][0] if site < 7 else 99
        for cell in sorted({key[0] for key in grid}):
            if cell < coming:
                flush(cell)


def spread_kernel(part_ref, table_ref, z_ref, send_ref, ball_ref):
    z_ref[...] = jnp.zeros_like(z_ref)
    pack_particles(part_ref, z_ref)
    spread_charges(z_ref, ball_ref)
    table = table_ref[...]
    for tile in range(5):
        rows = 128 if tile < 4 else 64
        result = matmul(table, ball_ref[tile * 128 : tile * 128 + rows, :], True)
        if rows < 128:
            result = jnp.concatenate([result, jnp.zeros((256, 128 - rows), f32)], axis=1)
        send_ref[:, tile, :] = result[0:128]
        send_ref[:, 5 + tile, :] = result[128:256]


def swap_quarters(parts):
    half = (lanes(parts[0].shape) >> 6) == 0
    quarter = ((lanes(parts[0].shape) >> 5) & 1) == 0
    a0 = jnp.where(half, parts[0], ahead(parts[2], 64))
    a2 = jnp.where(half, ahead(parts[0], 64), parts[2])
    a1 = jnp.where(half, parts[1], ahead(parts[3], 64))
    a3 = jnp.where(half, ahead(parts[1], 64), parts[3])
    b0 = jnp.where(quarter, a0, ahead(a1, -32))
    b1 = jnp.where(quarter, ahead(a0, 32), a1)
    b2 = jnp.where(quarter, a2, ahead(a3, -32))
    b3 = jnp.where(quarter, ahead(a2, 32), a3)
    return [b0, b1, b2, b3]


def middle_kernel(recv_ref, x_ref, xt_ref, y_ref, yt_ref, col_ref, row_ref, plane_ref, send_ref, both_ref):
    me = lax.axis_index("lane") * N_SLAB + lax.axis_index("slab")
    for half in range(2):
        for tile in range(5):
            parts = [recv_ref[lane * 32 : (lane + 1) * 32, half * 5 + tile, :] for lane in range(4)]
            swapped = swap_quarters(parts)
            for m in range(4):
                cell = 4 * tile + m
                if cell < WIN_X:
                    both_ref[cell * 32 : (cell + 1) * 32, half * 128 : (half + 1) * 128] = swapped[m]
    waves_x = matmul(x_ref[...], both_ref[...])
    back = []
    mine = plane_ref[pl.ds(me, 1)]
    for half in range(2):
        plane = matmul(waves_x[:, half * 128 : (half + 1) * 128], y_ref[...])
        sum_sq = col_ref[:, 1:2] + row_ref[1:2, :] + mine[0, half : half + 1, 1:2]
        gain = (col_ref[:, 0:1] * mine[0, half : half + 1, 0:1]) * row_ref[0:1, :]
        gain = jnp.where(sum_sq > 0.0, gain / jnp.where(sum_sq > 0.0, sum_sq, 1.0), 0.0)
        back.append(matmul(plane * gain, yt_ref[...]))
    both_ref[...] = matmul(xt_ref[...], jnp.concatenate(back, axis=1))
    for half in range(2):
        for tile in range(5):
            parts = []
            for m in range(4):
                cell = min(4 * tile + m, WIN_X - 1)
                parts.append(both_ref[cell * 32 : (cell + 1) * 32, half * 128 : (half + 1) * 128])
            swapped = swap_quarters(parts)
            for lane in range(4):
                send_ref[lane * 32 : (lane + 1) * 32, half * 5 + tile, :] = swapped[lane]


def interpolate(z_ref, pot_ref, o_ref):
    lane_cy = (lanes() >> 4) & 3
    sub = sublanes()

    def potential(cell, jz):
        row = (cell + 1) * 32
        value = pot_ref[row : row + 8, jz * 128 : (jz + 1) * 128]
        for cy in range(1, 4):
            other = pot_ref[row + 8 * cy : row + 8 * cy + 8, jz * 128 : (jz + 1) * 128]
            value = jnp.where(lane_cy == cy, other, value)
        return value

    held = {}
    for site in range(8):
        along_x, along_y, along_z, charge = site_offsets(z_ref, site)
        value_y, slope_y = spline(along_y, True)
        plain = [None] * 5
        sloped = [None] * 5
        for cell in X_WINDOWS[site]:
            value_x, slope_x = spline(along_x + (1.875 * (site + 0.5) - cell), True)
            for jz in range(5):
                key = (cell, jz)
                if key not in held:
                    held[key] = potential(cell, jz)
                sample = held[key]
                first = value_x * sample
                second = slope_x * sample
                plain[jz] = first if plain[jz] is None else plain[jz] + first
                sloped[jz] = second if sloped[jz] is None else sloped[jz] + second
        coming = X_WINDOWS[site + 1][0] if site < 7 else 99
        for key in [key for key in held if key[0] < coming]:
            del held[key]
        along = [None] * 3
        for jz in range(5):
            value_z, slope_z = spline(along_z + (2.0 - jz), True)
            terms = (sloped[jz] * value_z, plain[jz] * value_z, plain[jz] * slope_z)
            for axis in range(3):
                along[axis] = terms[axis] if along[axis] is None else along[axis] + terms[axis]
        scale = (
            value_y * charge * (-1.0 / HX),
            slope_y * charge * (-1.0 / HY),
            value_y * charge * (-1.0 / CELL_Z),
        )
        for axis in range(3):
            force = along[axis] * scale[axis]
            force = force + pltpu.roll(force, 4, axis=0)
            force = force + pltpu.roll(force, 2, axis=0)
            o_ref[0, site, axis : axis + 1, :] = force[0:1]
            o_ref[1, site, axis : axis + 1, :] = force[1:2]


def force_kernel(recv_ref, z_ref, table_ref, out_ref, pot_ref, o_ref):
    table = table_ref[...]
    for tile in range(5):
        rows = 128 if tile < 4 else 64
        left = jnp.concatenate([recv_ref[:, tile, :].T, recv_ref[:, 5 + tile, :].T], axis=1)
        pot_ref[tile * 128 : tile * 128 + rows, :] = matmul(left[0:rows], table)
    interpolate(z_ref, pot_ref, o_ref)
    unpack_forces(o_ref, out_ref)


def site_steps():
    steps = []
    for ez in (0, 1, -1):
        for ex in range(-5, 6):
            for ey in range(-5, 6):
                if ex == 0 and ey == 0 and ez == 0:
                    continue
                reach = 0.0
                for step, pitch in ((ex, SPACING), (ey, SPACING), (ez, SITE_Z)):
                    reach += max(abs(step) * pitch - 0.0601, 0.0) ** 2
                if reach < CUTOFF * CUTOFF:
                    steps.append((ex, ey, ez))
    return steps


STEPS = site_steps()
Y_RANGE = {0: range(-4, 6), 1: range(-2, 4), -1: range(-2, 4)}
SLOTS = {}
for _ez in (0, 1, -1):
    for _y in Y_RANGE[_ez]:
        SLOTS[(_y, _ez)] = len(SLOTS)


def near_kernel(center_ref, low_ref, high_ref, list_ref, count_ref, out_ref, ext_ref, o_ref):
    lane = lanes((16, 128))
    lane_cy = (lane >> 4) & 3
    lane_cz = lane & 15
    lane_az = lane >> 6
    x_row = sublanes((16, 128))
    shift_x = jnp.where(x_row < 4, -BRICK, jnp.where(x_row >= 12, BRICK, 0.0))

    for attr in range(6):
        own = [center_ref[parity, :, attr, :] for parity in range(2)]
        low = low_ref[:, attr, :]
        high = high_ref[:, attr, :]
        if attr == 0:
            own = [value + shift_x for value in own]
            low = low + shift_x
            high = high + shift_x
        if attr == 1:
            low = low - BRICK
            high = high + BRICK
        for y in Y_RANGE[0]:
            parity, step = y % 2, y // 2
            value = own[parity]
            if step > 0:
                value = jnp.where(
                    lane_cy + step >= 4, ahead(high, 16 * (step - 4 + 2 * parity)), ahead(value, 16 * step)
                )
            if step < 0:
                value = jnp.where(
                    lane_cy + step < 0, ahead(low, 16 * (step + 4 - 2 * parity)), ahead(value, 16 * step)
                )
            ext_ref[SLOTS[(y, 0)], attr] = value
            if y in Y_RANGE[1]:
                flipped = ahead(value, 64)
                up = jnp.where(lane_cz == 15, ahead(value, 49), ahead(value, 65))
                down = jnp.where(lane_cz == 0, ahead(value, 79), ahead(value, 63))
                if attr == 2:
                    up = jnp.where(lane_cz == 15, up + BOX_Z, up)
                    down = jnp.where(lane_cz == 0, down - BOX_Z, down)
                ext_ref[SLOTS[(y, 1)], attr] = jnp.where(lane_az == 0, flipped, up)
                ext_ref[SLOTS[(y, -1)], attr] = jnp.where(lane_az == 1, flipped, down)

    column = lax.broadcasted_iota(jnp.int32, (32, 256), 1)
    slot = lax.broadcasted_iota(jnp.int32, (32, 256), 0)
    entry = list_ref[...]
    brick = entry >> 8
    brick_x = jnp.where(brick >= 6, 2, jnp.where(brick >= 3, 1, 0))
    brick_y = brick - 3 * brick_x
    step_x = 4 * (brick_x - 1) + ((entry >> 6) & 3) - (column >> 6)
    step_y = 4 * (brick_y - 1) + ((entry >> 4) & 3) - ((column >> 4) & 3)
    step_z = ((entry & 15) - (column & 15)) & 15
    bit = jnp.left_shift(jnp.int32(1), 5 * (step_x + 2) + step_y + 2)
    bit = jnp.where(slot < count_ref[...], bit, 0)
    lane8 = lanes()
    row8 = sublanes()
    words = []
    for z_code in (0, 1, 15):
        chosen = jnp.where(step_z == z_code, bit, 0)
        total = chosen[0:8] + chosen[8:16] + chosen[16:24] + chosen[24:32]
        for turn in (4, 2, 1):
            total = total + pltpu.roll(total, turn, axis=0)
        word = None
        for pair in range(2):
            part = total[:, pair * 128 : (pair + 1) * 128]
            flipped = ahead(part, 64)
            even = jnp.where(lane8 < 64, part, flipped)
            odd = jnp.where(lane8 < 64, flipped, part)
            if word is None:
                word = jnp.where(row8 < 2, even, odd)
            else:
                word = jnp.where(row8 < 4, word, jnp.where(row8 < 6, even, odd))
        words.append(word)
    az8 = lane8 >> 6
    by_z = {
        0: words[0],
        1: jnp.where(az8 == 1, words[1], words[0]),
        -1: jnp.where(az8 == 0, words[2], words[0]),
    }
    odd_shift = 5 * (row8 & 1)
    by_z_odd = {key: jnp.right_shift(value, odd_shift) for key, value in by_z.items()}

    for ay in range(2):
        slot0 = SLOTS[(ay, 0)]
        own = [ext_ref[slot0, attr, 4:12, :] for attr in range(6)]
        own_six = own[4] * 6.0
        own_twelve = own[5] * 12.0
        total = [jnp.zeros((8, 128), f32) for _ in range(3)]
        for ex, ey, ez in STEPS:
            there = SLOTS[(ay + ey, ez)]
            far = [ext_ref[there, attr, 4 + ex : 12 + ex, :] for attr in range(6)]
            diff = [own[axis] - far[axis] for axis in range(3)]
            dist_sq = diff[0] * diff[0] + diff[1] * diff[1] + diff[2] * diff[2]
            root_inv = lax.rsqrt(dist_sq)
            inverse = root_inv * root_inv
            inverse_six = inverse * inverse * inverse
            dispersion = (own_twelve * far[5] * inverse_six - own_six * far[4]) * inverse_six
            ratio = 1.0 / (1.0 + (0.4 * EWALD_BETA) * (dist_sq * root_inv))
            scaled = jnp.full((8, 128), ERFCX[-1], f32)
            for factor in ERFCX[-2::-1]:
                scaled = scaled * ratio + factor
            gauss = jnp.exp(dist_sq * (-(EWALD_BETA**2)))
            coulomb = own[3] * far[3] * (gauss * (scaled * ratio * root_inv + 2.0 * EWALD_BETA / math.sqrt(math.pi)))
            switch = jnp.maximum(1.0 - dist_sq * (1.0 / (CUTOFF * CUTOFF)), 0.0)
            place = 5 * (ex // 2 + 2) + (ay + ey) // 2 + 2
            word = by_z_odd[ez] if ex % 2 else by_z[ez]
            listed = (word & (1 << place)) != 0
            scalar = jnp.where(listed, (dispersion + coulomb) * inverse * (switch * switch), 0.0)
            for axis in range(3):
                total[axis] = total[axis] + scalar * diff[axis]
        for axis in range(3):
            o_ref[ay, :, axis, :] = total[axis]
    unpack_forces(o_ref, out_ref)


def along(value, axis, step):
    count = lax.axis_size(axis)
    return lax.ppermute(value, axis, [(i, (i + step) % count) for i in range(count)])


def shards(table, particles, pair_list, pair_count):
    big = pltpu.CompilerParams(vmem_limit_bytes=48 * 1024 * 1024)
    packed, send = pl.pallas_call(
        spread_kernel,
        out_shape=(
            jax.ShapeDtypeStruct((4, 8, 8, 128), f32),
            jax.ShapeDtypeStruct((DEVICES, 10, 128), f32),
        ),
        in_specs=[VMEM] * 2,
        out_specs=(VMEM, VMEM),
        scratch_shapes=[pltpu.VMEM((576, 640), f32)],
        compiler_params=big,
    )(particles, table["z"])
    below = along(packed[:, 4:8], "slab", 1)
    above = along(packed[:, 0:4], "slab", -1)
    wide = jnp.concatenate([below, packed, above], axis=1)
    low = along(wide[2], "lane", 1)
    high = along(wide[3], "lane", -1)
    received = lax.all_to_all(send, ("lane", "slab"), split_axis=0, concat_axis=0, tiled=True)
    short_forces = pl.pallas_call(
        near_kernel,
        out_shape=jax.ShapeDtypeStruct((3, 2048), f32),
        in_specs=[VMEM] * 5,
        out_specs=VMEM,
        scratch_shapes=[
            pltpu.VMEM((len(SLOTS), 6, 16, 128), f32),
            pltpu.VMEM((2, 8, 8, 128), f32),
        ],
        compiler_params=big,
    )(wide[0:2], low, high, pair_list, pair_count.reshape(1, 256))
    outgoing = pl.pallas_call(
        middle_kernel,
        out_shape=jax.ShapeDtypeStruct((DEVICES, 10, 128), f32),
        in_specs=[VMEM] * 8,
        out_specs=VMEM,
        scratch_shapes=[pltpu.VMEM((576, 256), f32)],
        compiler_params=big,
    )(received, *(table[name] for name in ("x", "xt", "y", "yt", "col", "row", "plane")))
    returned = lax.all_to_all(outgoing, ("lane", "slab"), split_axis=0, concat_axis=0, tiled=True)
    long_forces = pl.pallas_call(
        force_kernel,
        out_shape=jax.ShapeDtypeStruct((3, 2048), f32),
        in_specs=[VMEM] * 3,
        out_specs=VMEM,
        scratch_shapes=[pltpu.VMEM((576, 640), f32), pltpu.VMEM((2, 8, 8, 128), f32)],
        compiler_params=big,
    )(returned, packed, table["z"])
    return short_forces, long_forces


def solution(mesh):
    table = tables()
    in_specs = (P(None, ("slab", "lane")), P(None, ("slab", "lane")), P(("slab", "lane")))
    out_specs = (P(None, ("slab", "lane")), P(None, ("slab", "lane")))
    body = functools.partial(shards, table)
    return jax.shard_map(body, mesh=mesh, in_specs=in_specs, out_specs=out_specs, check_vma=False)
```

time: 2290 us -> 79.4 us (0.03)
  local copies, waits for them, and re-layouts: 1380 us -> 3.28 us
  other arithmetic: 747 us -> 0 us
  matrix products: 68.5 us -> 0 us
    gather x4 -> x0, local copies, waits for them, and re-layouts: 795 us -> none  [the longest x2 725 us: shards(): sampled = widened_potential.reshape(-1)[padded_index]]
    scatter-add x1 -> x0, other arithmetic: 683 us -> none  [shards(): widened = jnp.zeros(GZ * wide_x * wide_y, jnp.float32).at[padded_index.re...]
    unnamed x65 -> x26, local copies, waits for them, and re-layouts: 269 us -> 3.24 us
    slice x14 -> x2, local copies, waits for them, and re-layouts: 106 us -> 0.02 us  [the longest x1 0.01 us: shards(): above = along(packed[:, 0:4], 'slab', -1)]
    reshape x6 -> x0, local copies, waits for them, and re-layouts: 94.2 us -> none  [the longest x1 78.8 us: shards(): outgoing = convolved.reshape(2, planes, num_slab, CELLS_X, num_lane, CELL...]
    all_to_all x3 -> x0, local copies, waits for them, and re-layouts: 65.5 us -> none  [the longest x2 65.4 us: shards(): lax.all_to_all(outgoing, ('slab', 'lane'), split_axis=2, concat_axis=1, t...]
    unnamed x12 -> x0, matrix products: 56.8 us -> none
    select_n x4 -> x0, other arithmetic: 24.6 us -> none  [the longest x2 23.8 us: pair_terms(): joined = jnp.take(nearby, slot_rows, axis=2)]
  transfers between devices with their start and end apart: 14 -> 6, of which waited for: 4 -> 4; matrix products, arithmetic and copies ran while one was open for 54% -> 0% of each run, Pallas kernels for 0% -> 15%
where the time goes in v1:
time: 79.4 us; the launch traced here: 79.1 us
  waiting for transfers between devices  33.3 us (42%)
  starting transfers between devices  22.9 us (29%)
  Pallas kernels  18.8 us (24%)
  local copies, waits for them, and re-layouts  3.28 us (4%)
    ppermute x4, waiting for transfers between devices, along(): lax.ppermute(value, axis, [(i, (i + step) % count) for i in range(count)])  17.6 us
    all_to_all x1, waiting for transfers between devices, shards(): lax.all_to_all(send, ('lane', 'slab'), split_axis=0, concat_axis=0, tiled...  15.7 us
    all_to_all x1, starting transfers between devices, shards(): lax.all_to_all(send, ('lane', 'slab'), split_axis=0, concat_axis=0, tiled...  10.8 us
    pallas_call x1, Pallas kernels, shards(): pl.pallas_call(middle_kernel, out_shape=jax.ShapeDtypeStruct((DEVICES, 10...  8.69 us
    all_to_all x1, starting transfers between devices, shards(): lax.all_to_all(outgoing, ('lane', 'slab'), split_axis=0, concat_axis=0, t...  6.91 us
    ppermute x4, starting transfers between devices, along(): lax.ppermute(value, axis, [(i, (i + step) % count) for i in range(count)])  5.21 us
    pallas_call x1, Pallas kernels, shards(): pl.pallas_call(spread_kernel, out_shape=(jax.ShapeDtypeStruct((4, 8, 8, 1...  4.14 us
    unnamed x26, local copies, waits for them, and re-layouts  3.24 us
  transfers between devices with their start and end apart: 6, of which 4 were waited for; matrix products, arithmetic and copies ran while one was open for 0% of the time, Pallas kernels for 15%

profile of v1, /device:TPU:5, one launch (start us, length us, event | category | flops | bytes accessed | tf_op | source)
XLA Modules:
  0.0 79.1 jit_solution(6020483279123246582)
XLA Ops:
  0.6 0.0 copy-start
  0.6 1.1 %copy-done = f32[256,640]{1,0:T(8,128)S(1)} copy-done((f32[256,640]{1,0:T(8,128)S(1)}, f32[256,640]{1,0:T(8,128)}, u32[]{:S(2)}) %copy-start) | copy-done | bytes 655384
  1.7 0.8 %copy-done.8 = f32[6,2048]{1,0:T(8,128)S(1)} copy-done((f32[6,2048]{1,0:T(8,128)S(1)}, f32[6,2048]{1,0:T(8,128)}, u32[]{:S(2)}) %copy-start.8) | copy-done | bytes 49176
  2.6 4.1 %shard_map.122 = (f32[4,8,8,128]{3,2,1,0:T(8,128)S(1)}, f32[128,10,128]{2,1,0:T(8,128)}) custom-call(f32[6,2048]{1,0:T(8,128)S(1)} %copy-done.8, f32[256,640]{1,0:T(8,128)S(1)} %copy-done), custom_call_target="tpu_custom_call" | custom-call | tf_op jit(solution)/shard_map/pallas_call | solution.py:479
  6.7 0.0 copy-start.7
  6.7 0.0 copy-start.10
  6.7 10.8 %all-to-all-start = ((f32[128,10,128]{2,1,0:T(8,128)}), f32[128,10,128]{2,1,0:T(8,128)S(1)}, u32[]{:S(2)}, u32[]{:S(2)}) async-start(f32[128,10,128]{2,1,0:T(8,128)} %get-tuple-element.5), calls=%async_computation | async-start | bytes 2097152 | tf_op jit(solution)/shard_map/all_to_all | solution.py:495
  17.6 1.5 %collective-permute-start = (f32[4,4,8,128]{3,2,1,0:T(8,128)S(1)}, f32[4,4,8,128]{3,2,1,0:T(8,128)S(1)}, u32[]{:S(2)}, u32[]{:S(2)}) collective-permute-start(f32[4,4,8,128]{3,2,1,0:T(8,128)S(1)} %get-tuple-element.9), channel_id=1, source_target_pairs={{0,4},{4,8},{8,12},{12,16},{16,20},{20,24},{24,28},{28,32},{32,36}... | collective-permute-start | bytes 196616 | tf_op jit(solution)/shard_map/ppermute | solution.py:474
  19.1 15.7 %all-to-all-done.recv_ref = f32[128,10,128]{2,1,0:T(8,128)S(1)} async-done(((f32[128,10,128]{2,1,0:T(8,128)}), f32[128,10,128]{2,1,0:T(8,128)S(1)}, u32[]{:S(2)}, u32[]{:S(2)}) %all-to-all-start) | async-done | bytes 655392 | tf_op jit(solution)/shard_map/all_to_all | solution.py:495
  34.8 0.0 copy-done.2
  34.8 0.0 copy-done.4
  34.8 0.0 copy-done.5
  34.8 0.0 copy-done.6
  34.8 0.0 copy-done.7
  34.8 0.0 copy-done.10
  34.8 0.0 copy-start.3
  34.8 1.3 %copy-done.3 = f32[576,480]{1,0:T(8,128)S(1)} copy-done((f32[576,480]{1,0:T(8,128)S(1)}, f32[576,480]{1,0:T(8,128)}, u32[]{:S(2)}) %copy-start.3) | copy-done | bytes 1105944
  36.1 8.7 %shard_map.124 = f32[128,10,128]{2,1,0:T(8,128)} custom-call(f32[128,10,128]{2,1,0:T(8,128)S(1)} %all-to-all-done.recv_ref, f32[480,576]{1,0:T(8,128)S(1)} %copy-done.2, f32[576,480]{1,0:T(8,128)S(1)} %copy-done.3, f32[128,160]{1,0:T(8,128)S(1)} %copy-done.6, f32[160,128]{1,0:T(8,128)S(1)} %copy-done.7, f32[480,2]{1,0:T(8,128)S(1)} %copy-done.4, ...), custom_call_target="tpu_custom_call" | custom-call | tf_op jit(solution)/shard_map/pallas_call | solution.py:507
  44.8 6.9 %all-to-all-start.1 = ((f32[128,10,128]{2,1,0:T(8,128)}), f32[128,10,128]{2,1,0:T(8,128)S(1)}, u32[]{:S(2)}, u32[]{:S(2)}) async-start(f32[128,10,128]{2,1,0:T(8,128)} %shard_map.124), calls=%async_computation.1 | async-start | bytes 2097152 | tf_op jit(solution)/shard_map/all_to_all | solution.py:515
  51.7 0.4 collective-permute-start.1
  52.1 0.0 collective-permute-done
  52.2 13.3 %collective-permute-done.1 = f32[4,4,8,128]{3,2,1,0:T(8,128)S(1)} collective-permute-done((f32[4,4,8,128]{3,2,1,0:T(8,128)S(1)}, f32[4,4,8,128]{3,2,1,0:T(8,128)S(1)}, u32[]{:S(2)}, u32[]{:S(2)}) %collective-permute-start.1) | collective-permute-done | bytes 65568 | tf_op jit(solution)/shard_map/ppermute | solution.py:474
  65.5 3.3 %collective-permute-start.3 = (f32[16,8,128]{2,1,0:T(8,128)S(1)}, f32[16,8,128]{2,1,0:T(8,128)S(1)}, u32[]{:S(2)}, u32[]{:S(2)}) collective-permute-start(f32[16,8,128]{2,1,0:T(8,128)S(1)} %get-tuple-element.6), channel_id=1, source_target_pairs={{0,3},{1,0},{2,1},{3,2},{4,7},{5,4},{6,5},{7,6},{8,11},{9,8},{10,9... | collective-permute-start | bytes 196616 | tf_op jit(solution)/shard_map/ppermute | solution.py:474
  68.8 0.0 collective-permute-start.2
  68.8 1.3 %collective-permute-done.3.high_ref = f32[16,8,128]{2,1,0:T(8,128)S(1)} collective-permute-done((f32[16,8,128]{2,1,0:T(8,128)S(1)}, f32[16,8,128]{2,1,0:T(8,128)S(1)}, u32[]{:S(2)}, u32[]{:S(2)}) %collective-permute-start.3) | collective-permute-done | bytes 65568 | tf_op jit(solution)/shard_map/ppermute | solution.py:474
  70.1 3.0 %collective-permute-done.2.low_ref = f32[16,8,128]{2,1,0:T(8,128)S(1)} collective-permute-done((f32[16,8,128]{2,1,0:T(8,128)S(1)}, f32[16,8,128]{2,1,0:T(8,128)S(1)}, u32[]{:S(2)}, u32[]{:S(2)}) %collective-permute-start.2) | collective-permute-done | bytes 65568 | tf_op jit(solution)/shard_map/ppermute | solution.py:474
  73.1 0.0 copy-done.9
  73.1 0.0 copy-done.11
  73.1 3.2 %shard_map.123 = f32[3,2048]{1,0:T(4,128)} custom-call(f32[2,16,8,128]{3,2,1,0:T(8,128)S(1)} %slice.20.center_ref, f32[16,8,128]{2,1,0:T(8,128)S(1)} %collective-permute-done.2.low_ref, f32[16,8,128]{2,1,0:T(8,128)S(1)} %collective-permute-done.3.high_ref, s32[32,256]{1,0:T(8,128)S(1)} %copy-done.9, s32[1,256]{1,0:T(1,128)S(1)} %bitcast.5), custom_call_target="tpu_custom_call" | custom-call | tf_op jit(solution)/shard_map/pallas_call | solution.py:496
  76.3 0.0 all-to-all-done.1.recv_ref
  76.3 0.0 copy-done.1
  76.3 2.7 %shard_map.125 = f32[3,2048]{1,0:T(4,128)} custom-call(f32[128,10,128]{2,1,0:T(8,128)S(1)} %all-to-all-done.1.recv_ref, f32[4,8,8,128]{3,2,1,0:T(8,128)S(1)} %get-tuple-element.4.z_ref, f32[256,640]{1,0:T(8,128)S(1)} %copy-done.1), custom_call_target="tpu_custom_call" | custom-call | tf_op jit(solution)/shard_map/pallas_call | solution.py:516
  (14 shorter events, 0.1 us)
Async XLA Ops:
  0.6 1.1 %copy-start = (f32[256,640]{1,0:T(8,128)S(1)}, f32[256,640]{1,0:T(8,128)}, u32[]{:S(2)}) copy-start(f32[256,640]{1,0:T(8,128)} %constant.16.clone.table_ref) | copy-start | bytes 1966084
  1.7 0.8 %copy-start.8 = (f32[6,2048]{1,0:T(8,128)S(1)}, f32[6,2048]{1,0:T(8,128)}, u32[]{:S(2)}) copy-start(f32[6,2048]{1,0:T(8,128)} %part_ref.1) | copy-start | bytes 147460
  6.7 28.1 %copy-start.2 = (f32[480,576]{1,0:T(8,128)S(1)}, f32[480,576]{1,0:T(8,128)}, u32[]{:S(2)}) copy-start(f32[480,576]{1,0:T(8,128)} %constant.17.clone.x_ref) | copy-start | bytes 3317764
  6.7 28.1 %copy-start.4 = (f32[480,2]{1,0:T(8,128)S(1)}, f32[480,2]{1,0:T(8,128)}, u32[]{:S(2)}) copy-start(f32[480,2]{1,0:T(8,128)} %constant.21.clone.col_ref) | copy-start | bytes 11524
  6.7 28.1 %copy-start.5 = (f32[128,2,2]{2,1,0:T(2,128)S(1)}, f32[128,2,2]{2,1,0:T(2,128)}, u32[]{:S(2)}) copy-start(f32[128,2,2]{2,1,0:T(2,128)} %constant.23.clone.plane_ref) | copy-start | bytes 6148
  6.7 28.1 %copy-start.6 = (f32[128,160]{1,0:T(8,128)S(1)}, f32[128,160]{1,0:T(8,128)}, u32[]{:S(2)}) copy-start(f32[128,160]{1,0:T(8,128)} %constant.19.clone.y_ref) | copy-start | bytes 245764
  6.7 28.1 %copy-start.7 = (f32[160,128]{1,0:T(8,128)S(1)}, f32[160,128]{1,0:T(8,128)}, u32[]{:S(2)}) copy-start(f32[160,128]{1,0:T(8,128)} %constant.20.clone.yt_ref) | copy-start | bytes 245764
  6.7 28.1 %copy-start.10 = (f32[2,160]{1,0:T(2,128)S(1)}, f32[2,160]{1,0:T(2,128)}, u32[]{:S(2)}) copy-start(f32[2,160]{1,0:T(2,128)} %constant.22.clone.row_ref) | copy-start | bytes 3844
  6.7 28.0 %all-to-all-start = ((f32[128,10,128]{2,1,0:T(8,128)}), f32[128,10,128]{2,1,0:T(8,128)S(1)}, u32[]{:S(2)}, u32[]{:S(2)}) async-start(f32[128,10,128]{2,1,0:T(8,128)} %get-tuple-element.5), calls=%async_computation | async-start | bytes 2097152 | tf_op jit(solution)/shard_map/all_to_all | solution.py:495
  17.6 34.6 %collective-permute-start = (f32[4,4,8,128]{3,2,1,0:T(8,128)S(1)}, f32[4,4,8,128]{3,2,1,0:T(8,128)S(1)}, u32[]{:S(2)}, u32[]{:S(2)}) collective-permute-start(f32[4,4,8,128]{3,2,1,0:T(8,128)S(1)} %get-tuple-element.9), channel_id=1, source_target_pairs={{0,4},{4,8},{8,12},{12,16},{16,20},{20,24},{24,28},{28,32},{32,36}... | collective-permute-start | bytes 196616 | tf_op jit(solution)/shard_map/ppermute | solution.py:474
  34.8 1.3 %copy-start.3 = (f32[576,480]{1,0:T(8,128)S(1)}, f32[576,480]{1,0:T(8,128)}, u32[]{:S(2)}) copy-start(f32[576,480]{1,0:T(8,128)} %constant.18.clone.xt_ref) | copy-start | bytes 3317764
  44.8 28.3 %copy-start.9 = (s32[32,256]{1,0:T(8,128)S(1)}, s32[32,256]{1,0:T(8,128)}, u32[]{:S(2)}) copy-start(s32[32,256]{1,0:T(8,128)} %list_ref.1) | copy-start | bytes 98308
  44.8 28.3 %copy-start.11 = (s32[256]{0:T(256)S(1)}, s32[256]{0:T(256)}, u32[]{:S(2)}) copy-start(s32[256]{0:T(256)} %param.13) | copy-start | bytes 3076
  44.8 31.6 %copy-start.1 = (f32[256,640]{1,0:T(8,128)S(1)}, f32[256,640]{1,0:T(8,128)}, u32[]{:S(2)}) copy-start(f32[256,640]{1,0:T(8,128)} %constant.16.clone.table_ref) | copy-start | bytes 1966084
  44.8 31.5 %all-to-all-start.1 = ((f32[128,10,128]{2,1,0:T(8,128)}), f32[128,10,128]{2,1,0:T(8,128)S(1)}, u32[]{:S(2)}, u32[]{:S(2)}) async-start(f32[128,10,128]{2,1,0:T(8,128)} %shard_map.124), calls=%async_computation.1 | async-start | bytes 2097152 | tf_op jit(solution)/shard_map/all_to_all | solution.py:515
  51.7 13.8 %collective-permute-start.1 = (f32[4,4,8,128]{3,2,1,0:T(8,128)S(1)}, f32[4,4,8,128]{3,2,1,0:T(8,128)S(1)}, u32[]{:S(2)}, u32[]{:S(2)}) collective-permute-start(f32[4,4,8,128]{3,2,1,0:T(8,128)S(1)} %get-tuple-element.8), channel_id=1, source_target_pairs={{0,124},{4,0},{8,4},{12,8},{16,12},{20,16},{24,20},{28,24},{32,28}... | collective-permute-start | bytes 196616 | tf_op jit(solution)/shard_map/ppermute | solution.py:474
  65.5 4.6 %collective-permute-start.3 = (f32[16,8,128]{2,1,0:T(8,128)S(1)}, f32[16,8,128]{2,1,0:T(8,128)S(1)}, u32[]{:S(2)}, u32[]{:S(2)}) collective-permute-start(f32[16,8,128]{2,1,0:T(8,128)S(1)} %get-tuple-element.6), channel_id=1, source_target_pairs={{0,3},{1,0},{2,1},{3,2},{4,7},{5,4},{6,5},{7,6},{8,11},{9,8},{10,9... | collective-permute-start | bytes 196616 | tf_op jit(solution)/shard_map/ppermute | solution.py:474
  68.8 4.3 %collective-permute-start.2 = (f32[16,8,128]{2,1,0:T(8,128)S(1)}, f32[16,8,128]{2,1,0:T(8,128)S(1)}, u32[]{:S(2)}, u32[]{:S(2)}) collective-permute-start(f32[16,8,128]{2,1,0:T(8,128)S(1)} %get-tuple-element.7), channel_id=1, source_target_pairs={{0,1},{1,2},{2,3},{3,0},{4,5},{5,6},{6,7},{7,4},{8,9},{9,10},{10,1... | collective-permute-start | bytes 196616 | tf_op jit(solution)/shard_map/ppermute | solution.py:474
